TPU v7x, 128 devices: a whole 4x4x4 slice. The times are simulated.
128 devices in a mesh: seq: 16 (over x_lo, z, core), fsdp: 8 (over y, x_hi).
Axes of the slice: x: 4 (x_hi: 2, x_lo: 2; x = x_hi * 2 + x_lo), y: 4, z: 4, core: 2. Of those that a mesh axis runs over, the one named last changes fastest.
Arguments:
- perturbed_codes: float32 [16, 1024, 2432], P('fsdp', 'seq'), may hold values from -6 to 6
- random_draws: float32 [2, 16, 1024, 2432], P(None, 'fsdp', 'seq'), may hold values from -6 to 6
- relative_rewards: float32 [16], P('fsdp'), may hold values from -4 to 4
- rescaling_gains: bfloat16 [2432], replicated, may hold values from 0.5 to 1.5
- triple_projector: bfloat16 [2432, 6144], P(None, 'seq'), may hold values from -2 to 2
- emission_projector: bfloat16 [2048, 2432], replicated, may hold values from -0.125 to 0.125
- payload_bypass_reducer: bfloat16 [2432, 32], replicated, may hold values from -0.125 to 0.125
- payload_bypass_lift: bfloat16 [32, 2048], replicated, may hold values from -1 to 1
- outlet_bypass_reducer: bfloat16 [2048, 32], replicated, may hold values from -0.125 to 0.125
- outlet_bypass_lift: bfloat16 [32, 2432], replicated, may hold values from -1 to 1
Outputs:
- ending_diffusion_image: float32 [16, 1024, 2432], P('fsdp', 'seq')
- grad_av: float32 [2432, 32], P(('seq', 'fsdp'))
- grad_bv: float32 [32, 2048], P(None, ('seq', 'fsdp'))
- outlet_reducer_derivative: float32 [2048, 32], P(('seq', 'fsdp'))
- output_up_gradient: float32 [32, 2432], P(None, ('seq', 'fsdp'))
All inputs are finite; a program needn't handle non-finite values.
Results may differ from a plain program's by a relative error of at most 0.017.
Values may be sent and summed in bfloat16 or wider, within the bound.
A program may use at most 192 MiB of HBM per device.

v0:
```python
import math

import jax
import jax.numpy as jnp
from jax import lax
from jax.experimental import pallas as pl
from jax.experimental.pallas import tpu as pltpu
from jax.sharding import PartitionSpec as P

TIMES = (0.8, 0.7)
STEP = -0.1
LEVEL = 0.7
EPS = 1e-06
SAMPLES = 16
WIDTH = 2432
INNER = 2048
RANK = 32
F32 = jnp.float32
BF16 = jnp.bfloat16
MESH = pl.DeviceIdType.MESH
NT = (((1,), (1,)), ((), ()))
TN = (((0,), (0,)), ((), ()))


def plan(index):
    moment = TIMES[index]
    sigma = LEVEL * math.sqrt(moment / (1.0 - moment))
    drift = sigma * sigma / (2.0 * moment)
    spread = sigma * math.sqrt(-STEP)
    keep = 1.0 + STEP * drift
    push = STEP * (1.0 + drift * (1.0 - moment))
    return (keep, push, spread)


def mm(a, b):
    return jnp.dot(a, b, preferred_element_type=F32)


def mm_nt(a, b):
    return lax.dot_general(a, b, NT, preferred_element_type=F32)


def mm_tn(a, b):
    return lax.dot_general(a, b, TN, preferred_element_type=F32)


def remote(src, dst, send, recv, device):
    return pltpu.make_async_remote_copy(
        src_ref=src,
        dst_ref=dst,
        send_sem=send,
        recv_sem=recv,
        device_id=device,
        device_id_type=MESH,
    )


def block_kernel(
    x_hbm, draws_hbm, rewards, gains, w_hbm, e_hbm, vred_t, vlift, ored_t, olift,
    x_out, sums_out,
    x0, draws, w_in, r2_sum, a_src, a_in, r_in, b_src, b_in,
    wall, ep, hid, kv, lowvt, dout, dsend, dlo, dlo_src, redp, lift2, lift3,
    att, att_src, dvel, dv, dlv, dl_src, dl_in, gav, gup,
    hs, hr, ks, kr, ds_, dr, ls, lr, as_, ar, ts, tr, ws, wr, es,
    s1, t1, s2, t2, s3, t3, ins,
):
    me = lax.axis_index("seq")
    fs = lax.axis_index("fsdp")
    x_lo, z, c = me // 8, (me // 2) % 4, me % 2
    y, x_hi = fs // 2, fs % 2
    group = z * 2 + c
    zp, zm, zo = (z + 1) % 4, (z + 3) % 4, (z + 2) % 4
    pending = []

    def col(zz, cc):
        return {"seq": (x_lo * 4 + zz) * 2 + cc, "fsdp": fs}

    def x_neighbour(step):
        xx = (x_hi * 2 + x_lo + step) % 4
        return {"seq": ((xx % 2) * 4 + z) * 2 + c, "fsdp": y * 2 + xx // 2}

    sibling = col(z, 1 - c)
    partner = {"seq": (me + 8) % 16, "fsdp": fs}

    def send(src, dst, s, r, device):
        copy = remote(src, dst, s, r, device)
        copy.start()
        pending.append(copy)

    def arrived(region, s, r):
        remote(region, region, s, r, sibling).wait_recv()

    w_load = pltpu.make_async_copy(w_hbm, w_in, ins.at[0])
    x_load = pltpu.make_async_copy(x_hbm, x0, ins.at[1])
    draws_load = pltpu.make_async_copy(draws_hbm, draws, ins.at[2])
    w_load.start()
    x_load.start()
    draws_load.start()

    loads = []
    for g in range(8):
        for h in range(2):
            copy = pltpu.make_async_copy(
                e_hbm.at[pl.ds(128 * (8 * h + g), 128), :],
                ep.at[pl.ds(256 * g + 128 * h, 128), :],
                es.at[2 * g + h],
            )
            copy.start()
            loads.append(copy)

    barrier = pltpu.get_barrier_semaphore()
    for d in range(1, 16):
        pl.semaphore_signal(
            barrier, inc=1, device_id={"seq": (me + d) % 16, "fsdp": fs}, device_id_type=MESH
        )
    outer = x_neighbour(jnp.where(x_lo == 0, -1, 1) + 4)
    pl.semaphore_signal(barrier, inc=1, device_id=outer, device_id_type=MESH)
    for d in range(1, 8):
        pl.semaphore_signal(
            barrier, inc=1, device_id={"seq": me, "fsdp": (fs + d) % 8}, device_id_type=MESH
        )

    low_half = lax.broadcasted_iota(jnp.int32, (128, 128), 1) < 64

    def w_columns(n, x):
        return pl.ds(pl.multiple_of(256 * n + 128 * x, 128), 128)

    def permute(i, _):
        rows = pl.ds(pl.multiple_of(i * 128, 128), 128)
        t0 = w_in[rows, 0:128].astype(F32)
        t1 = w_in[rows, 128:256].astype(F32)
        t2 = w_in[rows, 256:384].astype(F32)
        keys = pltpu.roll(jnp.where(low_half, t2, t0), 64, 1)
        wall[rows, w_columns(0, x_lo)] = (jnp.where(low_half, t0, t1) * 0.125).astype(BF16)
        wall[rows, w_columns(1, x_lo)] = keys.astype(BF16)
        wall[rows, w_columns(2, x_lo)] = jnp.where(low_half, t1, t2).astype(BF16)
        return 0

    w_load.wait()
    lax.fori_loop(0, WIDTH // 128, permute, 0)

    def hid_rows(k, s, zz, cc, start=0, size=64):
        return hid.at[k, s, pl.ds(pl.multiple_of(64 * (2 * zz + cc) + start, 32), size), :]

    own_rows = pl.ds(pl.multiple_of(64 * group, 64), 64)

    def norm(k, s, x):
        power = jnp.mean(x * x, axis=-1, keepdims=True)
        h = (x * lax.rsqrt(power + EPS) * gains[...].astype(F32)).astype(BF16)
        hid[k, s, own_rows, :] = h

    def gather_start(k, s):
        p = 2 * k + s
        own = hid_rows(k, s, z, c)
        send(own, own, hs.at[p, 1], hr.at[p, 1], col(zp, c))
        send(own, own, hs.at[p, 2], hr.at[p, 2], col(zm, c))
        send(own, own, hs.at[p, 0], hr.at[p, 0], sibling)

    def gather_near(k, s):
        p = 2 * k + s
        below, above = hid_rows(k, s, zm, c), hid_rows(k, s, zp, c)
        arrived(below, hs.at[p, 1], hr.at[p, 1])
        half = hid_rows(k, s, zm, c, 0, 32)
        send(half, half, hs.at[p, 4], hr.at[p, 4], col(zp, c))
        send(below, below, hs.at[p, 3], hr.at[p, 3], sibling)
        arrived(above, hs.at[p, 2], hr.at[p, 2])
        half = hid_rows(k, s, zp, c, 32, 32)
        send(half, half, hs.at[p, 6], hr.at[p, 6], col(zm, c))
        send(above, above, hs.at[p, 5], hr.at[p, 5], sibling)

    def gather_far(k, s):
        p = 2 * k + s
        for n, start in ((4, 0), (6, 32)):
            half = hid_rows(k, s, zo, c, start, 32)
            arrived(half, hs.at[p, n], hr.at[p, n])
            m = 7 if n == 4 else 8
            send(half, half, hs.at[p, m], hr.at[p, m], sibling)

    def project(k, s, j):
        p = 2 * k + s
        zz = (z, zm, zp, zo)[j]
        if j == 0:
            arrived(hid_rows(k, s, z, 1 - c), hs.at[p, 0], hr.at[p, 0])
        elif j == 1:
            arrived(hid_rows(k, s, zm, 1 - c), hs.at[p, 3], hr.at[p, 3])
        elif j == 2:
            arrived(hid_rows(k, s, zp, 1 - c), hs.at[p, 5], hr.at[p, 5])
        else:
            arrived(hid_rows(k, s, zo, 1 - c, 0, 32), hs.at[p, 7], hr.at[p, 7])
            arrived(hid_rows(k, s, zo, 1 - c, 32, 32), hs.at[p, 8], hr.at[p, 8])
        base = pl.multiple_of(128 * zz, 128)
        rows = pl.ds(base, 128)
        there = pl.ds(pl.multiple_of(x_lo * 512 + 128 * zz, 128), 128)
        low = mm_nt(hid[k, s, rows, :], vred_t[...])
        lowvt[k, s, x_lo, :, rows] = low.T.astype(BF16)
        lowb = low.astype(BF16)

        def third(i, _):
            lanes = pl.ds(pl.multiple_of(256 * i, 256), 256)
            mixed = mm(hid[k, s, rows, :], wall[:, lanes]) + mm(lowb, lift3[:, lanes])
            kv[k, s, there, lanes] = mixed.astype(BF16)
            return 0

        lax.fori_loop(0, 3, third, 0)
        region = kv.at[k, s, there, 256:768]
        send(region, region, ks.at[p, j], kr.at[p, j], partner)
        if j == 3:
            region = lowvt.at[k, s, x_lo]
            send(region, region, ks.at[p, 4], kr.at[p, 4], partner)

    def attention(k, s):
        p = 2 * k + s
        with jax.named_scope("keys_arrive"):
            for j in range(4):
                zz = (z, zm, zp, zo)[j]
                there = pl.ds(pl.multiple_of((1 - x_lo) * 512 + 128 * zz, 128), 128)
                arrived(kv.at[k, s, there, 256:768], ks.at[p, j], kr.at[p, j])
            arrived(lowvt.at[k, s, 1 - x_lo], ks.at[p, 4], kr.at[p, 4])
        lower = lax.broadcasted_iota(jnp.int32, (512, 128), 1) < 64
        queries = pl.ds(pl.multiple_of(x_lo * 512, 512), 512)
        for n in range(2):
            lanes = slice(128 * n, 128 * n + 128)
            q2 = kv[k, s, queries, lanes].astype(F32)
            do2 = dout[p, :, lanes].astype(F32)
            k2 = kv[k, s, :, 256 + 128 * n:384 + 128 * n]
            v2 = kv[k, s, :, 512 + 128 * n:640 + 128 * n]
            outs = []
            total = None
            for h in range(2):
                mask = lower if h == 0 else jnp.logical_not(lower)
                st = mm_nt(k2, jnp.where(mask, q2, 0.0).astype(BF16))
                e = jnp.exp(st - jnp.max(st, axis=0, keepdims=True))
                probs = (e * (1.0 / jnp.sum(e, axis=0, keepdims=True))).astype(BF16)
                outs.append(mm_tn(probs, v2))
                term = mm(probs, jnp.where(mask, do2, 0.0).astype(BF16))
                total = term if total is None else total + term
            dv[:, lanes] = total.astype(BF16)
            att_src[k, s, :, lanes] = jnp.where(lower, outs[0], outs[1]).astype(BF16)
            mine = pl.ds(pl.multiple_of(256 * group + 128 * n, 128), 128)
            for d in (4, 3, 5, 2, 6, 1, 7):
                g = (group + d) % 8
                send(
                    att_src.at[k, s, pl.ds(pl.multiple_of(64 * g, 64), 64), lanes],
                    att.at[k, s, :, mine],
                    as_.at[p, 8 * n + d],
                    ar.at[p, 8 * n + d],
                    {"seq": x_lo * 8 + g, "fsdp": fs},
                )
            att[k, s, :, mine] = att_src[k, s, own_rows, lanes]

    def values_gradient(k, s):
        dvb = dv[...]
        r2_sum[0:32, :] += mm(lowvt[k, s, 0], dvb[0:512]) + mm(lowvt[k, s, 1], dvb[512:1024])
        dlv[s] = mm_nt(lift2[...], dvb)

    def send_low_values(k):
        lower = lax.broadcasted_iota(jnp.int32, (32, 128), 1) < 64
        for j in range(8):
            b0, b1 = dlv[0, :, 128 * j:128 * j + 128], dlv[1, :, 128 * j:128 * j + 128]
            dl_src[k, 2 * j] = jnp.where(lower, b0, pltpu.roll(b1, 64, 1))
            dl_src[k, 2 * j + 1] = jnp.where(lower, pltpu.roll(b0, 64, 1), b1)
        for d in range(1, 16):
            to = (me + d) % 16
            send(
                dl_src.at[k, to], dl_in.at[k, d], ts.at[k, d], tr.at[k, d], {"seq": to, "fsdp": fs}
            )

    def reducer_gradient(k):
        total = jnp.zeros((32, 256), F32)
        for g in range(8):
            both = jnp.concatenate(
                [att_src[k, 0, 64 * g:64 * g + 64, :], att_src[k, 1, 64 * g:64 * g + 64, :]], axis=0
            )
            total = total + mm(dlo[g, 32 * k:32 * k + 32, :], both)
        r2_sum[32:64, :] += total

    def down_gradient(k):
        total = dl_src[k, me]
        for d in range(1, 16):
            arrived(dl_in.at[k, d], ts.at[k, d], tr.at[k, d])
            total = total + dl_in[k, d]
        both = jnp.concatenate([hid[k, 0, own_rows, :], hid[k, 1, own_rows, :]], axis=0)
        gav[...] += mm(total.astype(BF16), both)

    def outlet(k, s):
        p = 2 * k + s
        with jax.named_scope("heads_arrive"):
            for n in range(2):
                for d in range(1, 8):
                    g = (group + 8 - d) % 8
                    mine = pl.ds(pl.multiple_of(256 * g + 128 * n, 128), 128)
                    arrived(att.at[k, s, :, mine], as_.at[p, 8 * n + d], ar.at[p, 8 * n + d])
        keep, push, spread = plan(k)
        a = att[k, s]
        low = mm_nt(a, redp[...])
        lowb = low.astype(BF16)
        rows = slice(128 * k + 64 * s, 128 * k + 64 * s + 64)
        gup[...] += mm(low.T.astype(BF16), dvel[rows, :])
        def update(cols):
            v = mm(att[k, s], ep[:, cols]) + mm(lowb, olift[:, cols])
            old = x0[s, :, cols] if k == 0 else x_out[s, :, cols]
            x_out[s, :, cols] = keep * old + push * v + spread * draws[k, s, :, cols]

        def block(i, _):
            update(pl.ds(pl.multiple_of(512 * i, 512), 512))
            return 0

        lax.fori_loop(0, WIDTH // 512, block, 0)
        update(slice(WIDTH // 512 * 512, WIDTH))

    with jax.named_scope("entry"):
        pl.semaphore_wait(barrier, 23)
    half = WIDTH // 2
    for m in range(3):
        for n, step in ((0, 1), (1, 3)):
            region = wall.at[pl.ds(n * half, half), w_columns(m, x_lo)]
            send(region, region, ws.at[n, m], wr.at[n, m], x_neighbour(step))
    x_load.wait()
    with jax.named_scope("norm_0_0"):
        norm(0, 0, x0[0])
    with jax.named_scope("gather_start_0_0"):
        gather_start(0, 0)
    with jax.named_scope("norm_0_1"):
        norm(0, 1, x0[1])
    with jax.named_scope("gather_start_0_1"):
        gather_start(0, 1)
    draws_load.wait()

    lift2[:, 0:128] = vlift[:, pl.ds(pl.multiple_of(128 * group, 128), 128)]
    lift2[:, 128:256] = vlift[:, pl.ds(pl.multiple_of(1024 + 128 * group, 128), 128)]
    lift3[:, 0:512] = jnp.zeros((RANK, 512), BF16)
    lift3[:, 512:768] = lift2[...]
    for g in range(8):
        for h in range(2):
            redp[:, 256 * g + 128 * h:256 * g + 128 * h + 128] = ored_t[
                :, 128 * (8 * h + g):128 * (8 * h + g) + 128
            ]
    r2_sum[...] = jnp.zeros_like(r2_sum)
    gav[...] = jnp.zeros_like(gav)
    gup[...] = jnp.zeros_like(gup)

    for k in range(2):
        keep, push, spread = plan(k)
        coef = -push / (2.0 * SAMPLES * spread)
        for s in range(2):
            start = 128 * k + 64 * s
            dvel[start:start + 64, :] = ((coef * rewards[s]) * draws[k, s]).astype(BF16)
    with jax.named_scope("low_back"):
        low = mm_nt(dvel[...], olift[...])
        lowb = low.astype(BF16)
        low_t = low.T.astype(BF16)
        for k in range(2):
            dlo_src[32 * k:32 * k + 32, :] = low_t[:, 128 * k:128 * k + 128]

    for d in range(1, 8):
        g = (group + d) % 8
        send(dlo_src, dlo.at[group], ls.at[d], lr.at[d], {"seq": x_lo * 8 + g, "fsdp": fs})
    dlo[group] = dlo_src[...]

    with jax.named_scope("gather_near_0_0"):
        gather_near(0, 0)
    for copy in loads:
        copy.wait()

    def outlet_back(g, _):
        rows = pl.ds(pl.multiple_of(256 * g, 256), 256)
        d = mm_nt(dvel[...], ep[rows, :]) + mm(lowb, redp[:, rows])
        dsend[g] = d.astype(BF16).reshape(4, 64, 256)
        return 0

    def send_dout(k):
        steps = slice(2 * k, 2 * k + 2)
        for d in range(1, 8):
            g = (group + d) % 8
            send(
                dsend.at[g, steps],
                dout.at[steps, own_rows, :],
                ds_.at[k, d],
                dr.at[k, d],
                {"seq": x_lo * 8 + g, "fsdp": fs},
            )
        dout[steps, own_rows, :] = dsend[group, steps]

    def dout_arrives(k):
        for d in range(1, 8):
            g = (group + 8 - d) % 8
            rows = pl.ds(pl.multiple_of(64 * g, 64), 64)
            arrived(dout.at[2 * k:2 * k + 2, rows, :], ds_.at[k, d], dr.at[k, d])

    with jax.named_scope("outlet_back_low"):
        lax.fori_loop(0, 4, outlet_back, 0)
    with jax.named_scope("gather_far_0_0"):
        gather_far(0, 0)
    with jax.named_scope("outlet_back_high"):
        lax.fori_loop(4, 8, outlet_back, 0)
    with jax.named_scope("gather_near_0_1"):
        gather_near(0, 1)
    with jax.named_scope("projection_arrives"):
        for m in range(3):
            for n in range(2):
                region = wall.at[pl.ds(n * half, half), w_columns(m, 1 - x_lo)]
                arrived(region, ws.at[n, m], wr.at[n, m])
    with jax.named_scope("project_0_0_0"):
        project(0, 0, 0)
    with jax.named_scope("project_0_0_1"):
        project(0, 0, 1)
    with jax.named_scope("project_0_0_2"):
        project(0, 0, 2)
    with jax.named_scope("project_0_0_3"):
        project(0, 0, 3)
    with jax.named_scope("gather_far_0_1"):
        gather_far(0, 1)
    with jax.named_scope("send_dout_0"):
        send_dout(0)
    with jax.named_scope("project_0_1_0"):
        project(0, 1, 0)
    with jax.named_scope("project_0_1_1"):
        project(0, 1, 1)
    with jax.named_scope("project_0_1_2"):
        project(0, 1, 2)
    with jax.named_scope("project_0_1_3"):
        project(0, 1, 3)
    with jax.named_scope("send_dout_1"):
        send_dout(1)
    with jax.named_scope("dout_arrives_0"):
        dout_arrives(0)
    for d in range(1, 8):
        arrived(dlo.at[(group + 8 - d) % 8], ls.at[d], lr.at[d])
    with jax.named_scope("attention_0_0"):
        attention(0, 0)
    with jax.named_scope("values_gradient_0_0"):
        values_gradient(0, 0)
    with jax.named_scope("outlet_0_0"):
        outlet(0, 0)
    with jax.named_scope("norm_1_0"):
        norm(1, 0, x_out[0])
    with jax.named_scope("gather_start_1_0"):
        gather_start(1, 0)
    with jax.named_scope("project_1_0_0"):
        project(1, 0, 0)
    with jax.named_scope("attention_0_1"):
        attention(0, 1)
    with jax.named_scope("gather_near_1_0"):
        gather_near(1, 0)
    with jax.named_scope("project_1_0_1"):
        project(1, 0, 1)
    with jax.named_scope("project_1_0_2"):
        project(1, 0, 2)
    with jax.named_scope("values_gradient_0_1"):
        values_gradient(0, 1)
    with jax.named_scope("send_low_values_0"):
        send_low_values(0)
    with jax.named_scope("gather_far_1_0"):
        gather_far(1, 0)
    with jax.named_scope("project_1_0_3"):
        project(1, 0, 3)
    with jax.named_scope("outlet_0_1"):
        outlet(0, 1)
    with jax.named_scope("norm_1_1"):
        norm(1, 1, x_out[1])
    with jax.named_scope("gather_start_1_1"):
        gather_start(1, 1)
    with jax.named_scope("project_1_1_0"):
        project(1, 1, 0)
    with jax.named_scope("reducer_gradient_0"):
        reducer_gradient(0)
    with jax.named_scope("down_gradient_0"):
        down_gradient(0)
    with jax.named_scope("dout_arrives_1"):
        dout_arrives(1)
    with jax.named_scope("attention_1_0"):
        attention(1, 0)
    with jax.named_scope("gather_near_1_1"):
        gather_near(1, 1)
    with jax.named_scope("project_1_1_1"):
        project(1, 1, 1)
    with jax.named_scope("project_1_1_2"):
        project(1, 1, 2)
    with jax.named_scope("values_gradient_1_0"):
        values_gradient(1, 0)
    with jax.named_scope("gather_far_1_1"):
        gather_far(1, 1)
    with jax.named_scope("project_1_1_3"):
        project(1, 1, 3)
    with jax.named_scope("outlet_1_0"):
        outlet(1, 0)
    with jax.named_scope("attention_1_1"):
        attention(1, 1)
    with jax.named_scope("values_gradient_1_1"):
        values_gradient(1, 1)
    with jax.named_scope("send_low_values_1"):
        send_low_values(1)
    with jax.named_scope("reducer_gradient_1"):
        reducer_gradient(1)
    send(
        r2_sum.at[:, pl.ds(pl.multiple_of((1 - x_lo) * 128, 128), 128)], r_in, s2, t2, partner
    )
    with jax.named_scope("outlet_1_1"):
        outlet(1, 1)
    with jax.named_scope("down_gradient_1"):
        down_gradient(1)

    part = WIDTH // 16
    with jax.named_scope("wide_parts"):
        for t in range(16):
            a_src[t] = jnp.concatenate(
                [
                    gav[:, part * t:part * t + part],
                    gup[:, part * t:part * t + part],
                    jnp.zeros((RANK, 384 - 2 * part), F32),
                ],
                axis=1,
            ).astype(BF16)

    for d in range(1, 16):
        to = (me + d) % 16
        send(a_src.at[to], a_in.at[d], s1.at[d], t1.at[d], {"seq": to, "fsdp": fs})
    with jax.named_scope("sums_over_seq"):
        arrived(r_in, s2, t2)
    narrow = r2_sum[:, pl.ds(pl.multiple_of(x_lo * 128, 128), 128)] + r_in[...]
    with jax.named_scope("wide_sums"):
        total = a_src[me].astype(F32)
        for d in range(1, 16):
            arrived(a_in.at[d], s1.at[d], t1.at[d])
            total = total + a_in[d].astype(F32)

    step = part // 8
    with jax.named_scope("last_parts"):
        for f in range(8):
            b_src[f] = jnp.concatenate(
                [
                    total[:, step * f:step * f + step],
                    total[:, part + step * f:part + step * f + step],
                    narrow[0:32, 16 * f:16 * f + 16],
                    narrow[32:64, 16 * f:16 * f + 16],
                    jnp.zeros((RANK, 128 - 2 * step - 32), F32),
                ],
                axis=1,
            )

    for d in range(1, 8):
        to = (fs + d) % 8
        send(b_src.at[to], b_in.at[d], s3.at[d], t3.at[d], {"seq": me, "fsdp": to})
    with jax.named_scope("last_sums"):
        total = b_src[fs]
        for d in range(1, 8):
            arrived(b_in.at[d], s3.at[d], t3.at[d])
            total = total + b_in[d]

    sums_out[...] = total.T
    for copy in pending:
        copy.wait_send()


def per_device(
    perturbed_codes,
    random_draws,
    relative_rewards,
    rescaling_gains,
    triple_projector,
    emission_projector,
    payload_bypass_reducer,
    payload_bypass_lift,
    outlet_bypass_reducer,
    outlet_bypass_lift,
):
    vmem = pl.BlockSpec(memory_space=pltpu.VMEM)
    hbm = pl.BlockSpec(memory_space=pl.ANY)
    dma = pltpu.SemaphoreType.DMA
    final, sums = pl.pallas_call(
        block_kernel,
        out_shape=(
            jax.ShapeDtypeStruct((2, 64, WIDTH), F32),
            jax.ShapeDtypeStruct((128, RANK), F32),
        ),
        in_specs=[
            hbm, hbm, pl.BlockSpec(memory_space=pltpu.SMEM), vmem, hbm,
            hbm, vmem, vmem, vmem, vmem,
        ],
        out_specs=(vmem, vmem),
        scratch_shapes=[
            pltpu.VMEM((2, 64, WIDTH), F32),
            pltpu.VMEM((2, 2, 64, WIDTH), F32),
            pltpu.VMEM((WIDTH, 384), BF16),
            pltpu.VMEM((64, 256), F32),
            pltpu.VMEM((16, RANK, 384), BF16),
            pltpu.VMEM((16, RANK, 384), BF16),
            pltpu.VMEM((64, 128), F32),
            pltpu.VMEM((8, RANK, 128), F32),
            pltpu.VMEM((8, RANK, 128), F32),
            pltpu.VMEM((WIDTH, 768), BF16),
            pltpu.VMEM((INNER, WIDTH), BF16),
            pltpu.VMEM((2, 2, 512, WIDTH), BF16),
            pltpu.VMEM((2, 2, 1024, 768), BF16),
            pltpu.VMEM((2, 2, 2, RANK, 512), BF16),
            pltpu.VMEM((4, 512, 256), BF16),
            pltpu.VMEM((8, 4, 64, 256), BF16),
            pltpu.VMEM((8, 64, 128), BF16),
            pltpu.VMEM((64, 128), BF16),
            pltpu.VMEM((RANK, INNER), BF16),
            pltpu.VMEM((RANK, 256), BF16),
            pltpu.VMEM((RANK, 768), BF16),
            pltpu.VMEM((2, 2, 64, INNER), BF16),
            pltpu.VMEM((2, 2, 512, 256), BF16),
            pltpu.VMEM((256, WIDTH), BF16),
            pltpu.VMEM((1024, 256), BF16),
            pltpu.VMEM((2, RANK, 1024), F32),
            pltpu.VMEM((2, 16, RANK, 128), F32),
            pltpu.VMEM((2, 16, RANK, 128), F32),
            pltpu.VMEM((RANK, WIDTH), F32),
            pltpu.VMEM((RANK, WIDTH), F32),
            dma((4, 9)), dma((4, 9)),
            dma((4, 5)), dma((4, 5)),
            dma((2, 8)), dma((2, 8)),
            dma((8,)), dma((8,)),
            dma((4, 16)), dma((4, 16)),
            dma((2, 16)), dma((2, 16)),
            dma((2, 3)), dma((2, 3)),
            dma((16,)),
            dma((16,)), dma((16,)),
            dma, dma,
            dma((8,)), dma((8,)),
            dma((3,)),
        ],
        compiler_params=pltpu.CompilerParams(
            collective_id=0, has_side_effects=True, vmem_limit_bytes=58 * 1024 * 1024
        ),
        name="rollout",
    )(
        perturbed_codes,
        random_draws,
        relative_rewards,
        rescaling_gains.reshape(1, WIDTH),
        triple_projector,
        emission_projector,
        payload_bypass_reducer.T,
        payload_bypass_lift,
        outlet_bypass_reducer.T,
        outlet_bypass_lift,
    )
    wide, narrow = WIDTH // 128, INNER // 128
    ends = (0, wide, 2 * wide, 2 * wide + narrow, 2 * wide + 2 * narrow)
    gav, gup, gbv, gred = (sums[a:b] for a, b in zip(ends, ends[1:]))
    return (final, gav, gbv.T, gred, gup.T)


def solution(mesh):
    placed = (
        P("fsdp", "seq", None),
        P(None, "fsdp", "seq", None),
        P("fsdp"),
        P(),
        P(None, "seq"),
        P(),
        P(),
        P(),
        P(),
        P(),
    )
    return jax.shard_map(
        per_device,
        mesh=mesh,
        in_specs=placed,
        out_specs=(
            P("fsdp", "seq", None),
            P(("seq", "fsdp"), None),
            P(None, ("seq", "fsdp")),
            P(("seq", "fsdp"), None),
            P(None, ("seq", "fsdp")),
        ),
        check_vma=False,
    )
```

profile of v0, /device:TPU:1, one launch (start us, length us, event | category | flops | bytes accessed | tf_op | source)
XLA Modules:
  0.0 146.3 jit_solution(1275594510997780814)
XLA Ops:
  0.6 1.3 reshape.13.gains
  1.9 139.2 %rollout.1 = (f32[2,64,2432]{2,1,0:T(8,128)}, f32[128,32]{1,0:T(8,128)}) custom-call(f32[2,64,2432]{2,1,0:T(8,128)} %x_hbm.1, f32[2,2,64,2432]{3,2,1,0:T(8,128)} %draws_hbm.1, f32[2]{0:T(128)} %rewards.1, bf16[1,2432]{1,0:T(2,128)(2,1)} %reshape.13.gains, bf16[2432,384]{1,0:T(8,128)(2,1)} %w_hbm.1, bf16[2048,2432]{1,0:T(8,128)(2,1)} %e_hbm.1, ...), custom_call_target="tpu_custom_call" | custom-call | tf_op jit(solution)/shard_map/rollout/pallas_call | solution.py:570
  141.1 1.4 slice_bitcast_fusion
  142.5 1.4 fusion
  143.9 2.4 %copy.16 = f32[2,64,2432]{2,1,0:T(8,128)} copy(f32[2,64,2432]{2,1,0:T(8,128)} %get-tuple-element.18) | data formatting | bytes 2490368
where the time goes:
time: 147 us; the launch traced here: 146 us
  Pallas kernels  139 us (95%)
  local copies, waits for them, and re-layouts  6.48 us (4%)
    pallas_call x1, Pallas kernels, per_device(): pl.pallas_call(block_kernel, out_shape=(jax.ShapeDtypeStruct((2, 64, WIDT...  139 us

commit v1 on v0

--- a/solution.py
+++ b/solution.py
@@ -146,7 +146,7 @@
 
     def norm(k, s, x):
         power = jnp.mean(x * x, axis=-1, keepdims=True)
-        h = (x * lax.rsqrt(power + EPS) * gains[...].astype(F32)).astype(BF16)
+        h = (x * lax.rsqrt(power + EPS) * gains[...].astype(F32)[None, :]).astype(BF16)
         hid[k, s, own_rows, :] = h
 
     def gather_start(k, s):
@@ -630,7 +630,7 @@
         perturbed_codes,
         random_draws,
         relative_rewards,
-        rescaling_gains.reshape(1, WIDTH),
+        rescaling_gains,
         triple_projector,
         emission_projector,
         payload_bypass_reducer.T,

time: 147 us -> 145 us (0.986)
  no operation moved by 1% of the time
where the time goes in v1:
time: 145 us
  Pallas kernels  139 us (96%)
  local copies, waits for them, and re-layouts  5.19 us (4%)
    pallas_call x1, Pallas kernels, per_device(): pl.pallas_call(block_kernel, out_shape=(jax.ShapeDtypeStruct((2, 64, WIDT...  139 us

profile of v1, /device:TPU:1, one launch (start us, length us, event | category | flops | bytes accessed | tf_op | source)
XLA Modules:
  0.0 145.0 jit_solution(73649241249079575)
XLA Ops:
  0.6 139.2 %rollout.1 = (f32[2,64,2432]{2,1,0:T(8,128)}, f32[128,32]{1,0:T(8,128)}) custom-call(f32[2,64,2432]{2,1,0:T(8,128)} %x_hbm.1, f32[2,2,64,2432]{3,2,1,0:T(8,128)} %draws_hbm.1, f32[2]{0:T(128)} %rewards.1, bf16[2432]{0:T(1024)(128)(2,1)} %gains.1, bf16[2432,384]{1,0:T(8,128)(2,1)} %w_hbm.1, bf16[2048,2432]{1,0:T(8,128)(2,1)} %e_hbm.1, ...), custom_call_target="tpu_custom_call" | custom-call | tf_op jit(solution)/shard_map/rollout/pallas_call | solution.py:570
  139.8 1.4 slice_bitcast_fusion
  141.2 1.4 fusion
  142.6 2.4 %copy.16 = f32[2,64,2432]{2,1,0:T(8,128)} copy(f32[2,64,2432]{2,1,0:T(8,128)} %get-tuple-element.18) | data formatting | bytes 2490368

commit v2 on v1

--- a/solution.py
+++ b/solution.py
@@ -497,40 +497,50 @@
     )
     with jax.named_scope("outlet_1_1"):
         outlet(1, 1)
+    part = WIDTH // 16
+
+    def send_wide(n, grad):
+        for t in range(16):
+            a_src[n, t] = jnp.concatenate(
+                [grad[:, part * t:part * t + part], jnp.zeros((RANK, 256 - part), F32)], axis=1
+            ).astype(BF16)
+        for d in range(1, 16):
+            to = (me + d) % 16
+            send(
+                a_src.at[n, to],
+                a_in.at[n, d],
+                s1.at[n, d],
+                t1.at[n, d],
+                {"seq": to, "fsdp": fs},
+            )
+
+    def wide_sum(n):
+        total = a_src[n, me].astype(F32)
+        for d in range(1, 16):
+            arrived(a_in.at[n, d], s1.at[n, d], t1.at[n, d])
+            total = total + a_in[n, d].astype(F32)
+        return total
+
+    with jax.named_scope("send_wide_up"):
+        send_wide(1, gup)
     with jax.named_scope("down_gradient_1"):
         down_gradient(1)
-
-    part = WIDTH // 16
-    with jax.named_scope("wide_parts"):
-        for t in range(16):
-            a_src[t] = jnp.concatenate(
-                [
-                    gav[:, part * t:part * t + part],
-                    gup[:, part * t:part * t + part],
-                    jnp.zeros((RANK, 384 - 2 * part), F32),
-                ],
-                axis=1,
-            ).astype(BF16)
-
-    for d in range(1, 16):
-        to = (me + d) % 16
-        send(a_src.at[to], a_in.at[d], s1.at[d], t1.at[d], {"seq": to, "fsdp": fs})
+    with jax.named_scope("send_wide_down"):
+        send_wide(0, gav)
     with jax.named_scope("sums_over_seq"):
         arrived(r_in, s2, t2)
     narrow = r2_sum[:, pl.ds(pl.multiple_of(x_lo * 128, 128), 128)] + r_in[...]
     with jax.named_scope("wide_sums"):
-        total = a_src[me].astype(F32)
-        for d in range(1, 16):
-            arrived(a_in.at[d], s1.at[d], t1.at[d])
-            total = total + a_in[d].astype(F32)
+        up_sum = wide_sum(1)
+        down_sum = wide_sum(0)
 
     step = part // 8
     with jax.named_scope("last_parts"):
         for f in range(8):
             b_src[f] = jnp.concatenate(
                 [
-                    total[:, step * f:step * f + step],
-                    total[:, part + step * f:part + step * f + step],
+                    down_sum[:, step * f:step * f + step],
+                    up_sum[:, step * f:step * f + step],
                     narrow[0:32, 16 * f:16 * f + 16],
                     narrow[32:64, 16 * f:16 * f + 16],
                     jnp.zeros((RANK, 128 - 2 * step - 32), F32),
@@ -583,8 +593,8 @@
             pltpu.VMEM((2, 2, 64, WIDTH), F32),
             pltpu.VMEM((WIDTH, 384), BF16),
             pltpu.VMEM((64, 256), F32),
-            pltpu.VMEM((16, RANK, 384), BF16),
-            pltpu.VMEM((16, RANK, 384), BF16),
+            pltpu.VMEM((2, 16, RANK, 256), BF16),
+            pltpu.VMEM((2, 16, RANK, 256), BF16),
             pltpu.VMEM((64, 128), F32),
             pltpu.VMEM((8, RANK, 128), F32),
             pltpu.VMEM((8, RANK, 128), F32),
@@ -617,7 +627,7 @@
             dma((2, 16)), dma((2, 16)),
             dma((2, 3)), dma((2, 3)),
             dma((16,)),
-            dma((16,)), dma((16,)),
+            dma((2, 16)), dma((2, 16)),
             dma, dma,
             dma((8,)), dma((8,)),
             dma((3,)),

time: 145 us -> 147 us (1.014)
  Pallas kernels: 139 us -> 141 us
where the time goes in v2:
time: 147 us; the launch traced here: 146 us
  Pallas kernels  141 us (96%)
  local copies, waits for them, and re-layouts  5.19 us (4%)
    pallas_call x1, Pallas kernels, per_device(): pl.pallas_call(block_kernel, out_shape=(jax.ShapeDtypeStruct((2, 64, WIDT...  141 us

profile of v2, /device:TPU:1, one launch (start us, length us, event | category | flops | bytes accessed | tf_op | source)
XLA Modules:
  0.0 146.4 jit_solution(12476845232825022140)
XLA Ops:
  0.6 140.6 %rollout.1 = (f32[2,64,2432]{2,1,0:T(8,128)}, f32[128,32]{1,0:T(8,128)}) custom-call(f32[2,64,2432]{2,1,0:T(8,128)} %x_hbm.1, f32[2,2,64,2432]{3,2,1,0:T(8,128)} %draws_hbm.1, f32[2]{0:T(128)} %rewards.1, bf16[2432]{0:T(1024)(128)(2,1)} %gains.1, bf16[2432,384]{1,0:T(8,128)(2,1)} %w_hbm.1, bf16[2048,2432]{1,0:T(8,128)(2,1)} %e_hbm.1, ...), custom_call_target="tpu_custom_call" | custom-call | tf_op jit(solution)/shard_map/rollout/pallas_call | solution.py:580
  141.2 1.4 slice_bitcast_fusion
  142.6 1.4 fusion
  144.0 2.4 %copy.16 = f32[2,64,2432]{2,1,0:T(8,128)} copy(f32[2,64,2432]{2,1,0:T(8,128)} %get-tuple-element.18) | data formatting | bytes 2490368
